TPU v7x, 32 devices: a whole 2x2x4 slice. The times are simulated.
32 devices in a mesh: sec: 4 (over y, core), blk: 8 (over z, x).
Axes of the slice: x: 2, y: 2, z: 4, core: 2. Of those that a mesh axis runs over, the one named last changes fastest.
Arguments:
- left_built: bfloat16 [4, 6, 16, 256, 256], P('sec', None, 'blk'), may hold values from -0.375 to 0.375
- right_env: bfloat16 [4, 6, 16, 256, 256], P('sec', None, 'blk'), may hold values from -0.375 to 0.375
- psi_init: float32 [4, 16, 256, 256], P('sec', 'blk')
- block_dims: int32 [4, 16], P('sec', 'blk'), may hold values from 64 to 256, as said below
- ranks: int32 [4, 16], P('sec', 'blk'), may hold values from 2 to 128, as said below
- sketch: float32 [4, 16, 256, 128], P('sec', 'blk'), may hold values from -6 to 6
Outputs:
- truncated: float32 [4, 16, 256, 256], P('sec', 'blk')
- alphas: float32 [4, 4], P('sec')
- betas: float32 [4, 4], P('sec')
Inputs may be any that keep to these rules, and one draw needn't show every extreme that they name: `block_dims`: in each section at least one block has dimension exactly 256. `ranks`: each rank is at most half of its block's dimension; in each section at least one block of dimension 256 has rank 256 // 2.
All inputs are finite; a program needn't handle non-finite values.
Results may differ from a plain program's by a relative error of at most 0.0096.
Values may be sent and summed in bfloat16 or wider, within the bound.
A program may use at most 64 MiB of HBM per device.

v0:
```python
import jax
import jax.numpy as jnp
from jax import lax
from jax.sharding import PartitionSpec as P

STEPS = 4


def passed_along(block, axis, distance):
    devices = range(lax.axis_size(axis))
    route = [((i - distance) % len(devices), i) for i in devices]
    return lax.ppermute(block, axis, route)


def with_halo(cells, sides, width):
    for axis, dim in sides:
        count = lax.axis_size(axis)
        ends = count - 1
        head = lax.slice_in_dim(cells, 0, width, axis=dim)
        tail = lax.slice_in_dim(cells, cells.shape[dim] - width, cells.shape[dim], axis=dim)
        cells = jnp.concatenate(
            [
                lax.ppermute(tail, axis, [(i, (i + 1) % count) for i in range(ends)]),
                cells,
                lax.ppermute(head, axis, [((i + 1) % count, i) for i in range(ends)]),
            ],
            axis=dim,
        )
    return cells


def project_block(blockv, sketchb, cmask):
    hp = lax.Precision.HIGHEST
    ymat = jnp.dot(blockv, sketchb, precision=hp) * cmask[None, :]
    gram = jnp.dot(ymat.T, ymat, precision=hp) + jnp.diag(1.0 - cmask)
    factor = jnp.linalg.cholesky(gram)
    rhs = jnp.dot(ymat.T, blockv, precision=hp)
    inner = lax.linalg.triangular_solve(factor, rhs, left_side=True, lower=True)
    coef = lax.linalg.triangular_solve(factor, inner, left_side=True, lower=True, transpose_a=True)
    return jnp.dot(ymat, coef, precision=hp)


def shards(left_built, right_env, psi_init, block_dims, ranks, sketch):
    blocks = psi_init.shape[1]
    side = psi_init.shape[2]
    terms = right_env.shape[1]
    count = float(lax.axis_size("blk") * blocks * side * side)
    right = right_env[0]
    left = passed_along(left_built, "sec", 1)[0]
    left_terms = [left[k] for k in range(terms)]
    dims = block_dims[0]
    iota = jnp.arange(side)
    rowmask = (iota[None, :] < dims[:, None]).astype(jnp.float32)
    cellmask = rowmask[:, :, None] * rowmask[:, None, :]
    vec = psi_init[0] * cellmask
    start_sq = lax.psum(jnp.sum(vec * vec), "blk")
    vec = vec * jnp.sqrt(count / start_sq)
    prev = jnp.zeros_like(vec)
    beta = jnp.float32(0.0)
    alpha_list = []
    beta_list = []
    for step in range(STEPS):
        ext = with_halo(vec.astype(jnp.bfloat16), (("blk", 0),), blocks)
        lower = ext[:blocks]
        own = ext[blocks : 2 * blocks]
        upper = ext[2 * blocks :]
        blank = jnp.zeros((1, side, side), jnp.bfloat16)
        down = jnp.concatenate([blank, lower[:-1]], 0)
        rise = jnp.concatenate([upper[1:], blank], 0)
        sources = [own, own, lower, upper, down, rise]
        total = jnp.zeros((blocks, side, side), jnp.float32)
        for apply_k in range(terms):
            mixed = jnp.einsum(
                "jab,jcb->jac", sources[apply_k], right[apply_k], preferred_element_type=jnp.float32
            ).astype(jnp.bfloat16)
            total = total + jnp.einsum(
                "jab,jbc->jac", left_terms[apply_k], mixed, preferred_element_type=jnp.float32
            )
        image = total * cellmask
        alpha = lax.psum(jnp.sum(vec * image), "blk") / count
        resid = image - alpha * vec - beta * prev
        resid_sq = lax.psum(jnp.sum(resid * resid), "blk")
        beta = jnp.sqrt(resid_sq / count + 1e-06)
        prev = vec
        vec = resid / beta
        alpha_list.append(alpha)
        beta_list.append(beta)
    rmax = sketch.shape[3]
    cmask = (jnp.arange(rmax)[None, :] < ranks[0][:, None]).astype(jnp.float32)
    truncated = jax.vmap(project_block)(vec, sketch[0], cmask)
    alphas = jnp.stack(alpha_list).reshape(1, STEPS)
    betas = jnp.stack(beta_list).reshape(1, STEPS)
    return (truncated[None], alphas, betas)


def solution(mesh):
    placed = (
        P("sec", None, "blk", None, None),
        P("sec", None, "blk", None, None),
        P("sec", "blk", None, None),
        P("sec", "blk"),
        P("sec", "blk"),
        P("sec", "blk", None, None),
    )
    return jax.shard_map(
        shards,
        mesh=mesh,
        in_specs=placed,
        out_specs=(P("sec", "blk", None, None), P("sec", None), P("sec", None)),
        check_vma=False,
    )
```

profile of v0, /device:TPU:0, one launch (start us, length us, event | category | flops | bytes accessed | tf_op | source)
XLA Modules:
  0.0 338.5 jit_solution(1910883809504886635)
XLA Ops:
  3.9 23.3 %psum.63 = f32[]{:T(128)} all-reduce(f32[]{:T(128)} %multiply_reduce_fusion.8), channel_id=1, replica_groups=mesh['sec'=4,'blk'=8] {'blk'}, use_global_device_ids=true, to_apply=%region_1.0 | all-reduce | flops 1 | bytes 8 | tf_op jit(solution)/shard_map/psum | solution.py:56
  29.4 4.6 %collective-permute-start.1 = (bf16[2,256,256]{1,2,0:T(8,128)(2,1)S(1)}, bf16[2,256,256]{1,2,0:T(8,128)(2,1)S(1)}, u32[]{:S(2)}, u32[]{:S(2)}) collective-permute-start(bf16[2,256,256]{1,2,0:T(8,128)(2,1)S(1)} %fusion.106), channel_id=1, source_target_pairs={{0,1},{1,2},{2,3},{3,4},{4,5},{5,6},{6,7},{8,9},{9,10},{10,11},{11... | collective-permute-start | bytes 786440 | tf_op jit(solution)/shard_map/ppermute | solution.py:23
  34.0 2.4 collective-permute-done.2
  38.3 2.1 fusion.22
  40.4 2.1 fusion.21
  42.5 2.1 fusion.20
  48.8 2.8 multiply_reduce_fusion.7
  51.7 20.2 %psum.64 = f32[]{:T(128)} all-reduce(f32[]{:T(128)} %get-tuple-element.11), channel_id=1, replica_groups=mesh['sec'=4,'blk'=8] {'blk'}, use_global_device_ids=true, to_apply=%region_3.0 | all-reduce | flops 1 | bytes 8 | tf_op jit(solution)/shard_map/psum | solution.py:80
  73.5 17.8 %psum.65 = f32[]{:T(128)} all-reduce(f32[]{:T(128)} %multiply_reduce_fusion.6), channel_id=1, replica_groups=mesh['sec'=4,'blk'=8] {'blk'}, use_global_device_ids=true, to_apply=%region_5.0 | all-reduce | flops 1 | bytes 8 | tf_op jit(solution)/shard_map/psum | solution.py:82
  94.3 5.7 %collective-permute-start.3 = (bf16[2,256,256]{1,2,0:T(8,128)(2,1)}, bf16[2,256,256]{1,2,0:T(8,128)(2,1)S(1)}, u32[]{:S(2)}, u32[]{:S(2)}) collective-permute-start(bf16[2,256,256]{1,2,0:T(8,128)(2,1)} %get-tuple-element.9), channel_id=1, source_target_pairs={{0,1},{1,2},{2,3},{3,4},{4,5},{5,6},{6,7},{8,9},{9,10},{10,11},{11... | collective-permute-start | bytes 786440 | tf_op jit(solution)/shard_map/ppermute | solution.py:23
  99.9 2.2 fusion.25
  102.5 2.1 fusion.27
  105.8 2.1 fusion.26
  112.2 2.9 multiply_reduce_fusion.5
  115.1 20.1 %psum.66 = f32[]{:T(128)} all-reduce(f32[]{:T(128)} %get-tuple-element.13), channel_id=1, replica_groups=mesh['sec'=4,'blk'=8] {'blk'}, use_global_device_ids=true, to_apply=%region_7.0 | all-reduce | flops 1 | bytes 8 | tf_op jit(solution)/shard_map/psum | solution.py:80
  137.5 17.7 %psum.67 = f32[]{:T(128)} all-reduce(f32[]{:T(128)} %get-tuple-element.7), channel_id=1, replica_groups=mesh['sec'=4,'blk'=8] {'blk'}, use_global_device_ids=true, to_apply=%region_9.0 | all-reduce | flops 1 | bytes 8 | tf_op jit(solution)/shard_map/psum | solution.py:82
  159.6 5.4 %collective-permute-start.5 = (bf16[2,256,256]{1,2,0:T(8,128)(2,1)}, bf16[2,256,256]{1,2,0:T(8,128)(2,1)}, u32[]{:S(2)}, u32[]{:S(2)}) collective-permute-start(bf16[2,256,256]{1,2,0:T(8,128)(2,1)} %fusion.179), channel_id=1, source_target_pairs={{0,1},{1,2},{2,3},{3,4},{4,5},{5,6},{6,7},{8,9},{9,10},{10,11},{11... | collective-permute-start | bytes 786440 | tf_op jit(solution)/shard_map/ppermute | solution.py:23
  165.0 2.2 fusion.30
  168.1 2.1 fusion.32
  171.8 2.1 fusion.31
  177.1 3.8 %multiply_reduce_fusion.3 = (f32[]{:T(128)}, f32[2,256,256]{1,2,0:T(8,128)}) fusion(f32[2,256,256]{1,2,0:T(8,128)} %get-tuple-element.8, f32[]{:T(128)} %sqrt.17, f32[2,256]{1,0:T(2,128)S(1)} %compare_convert_fusion, f32[2,256,256]{2,1,0:T(8,128)} %fusion.34, f32[2,256,256]{2,1,0:T(8,128)} %fusion.33, f32[2,256,256]{2,1,0:T(8,128)} %fusion.32, ...), kind=kOutput, calls=%fused_computation.80 | convolution fusion | flops 135659520 | bytes 4460552 | tf_op jit(solution)/shard_map/jab,jbc->jac/dot_general | solution.py:76
  180.9 20.0 %psum.68 = f32[]{:T(128)} all-reduce(f32[]{:T(128)} %get-tuple-element.15), channel_id=1, replica_groups=mesh['sec'=4,'blk'=8] {'blk'}, use_global_device_ids=true, to_apply=%region_11.0 | all-reduce | flops 1 | bytes 8 | tf_op jit(solution)/shard_map/psum | solution.py:80
  201.5 2.9 multiply_reduce_fusion.2
  204.4 17.7 %psum.69 = f32[]{:T(128)} all-reduce(f32[]{:T(128)} %get-tuple-element.5), channel_id=1, replica_groups=mesh['sec'=4,'blk'=8] {'blk'}, use_global_device_ids=true, to_apply=%region_13.0 | all-reduce | flops 1 | bytes 8 | tf_op jit(solution)/shard_map/psum | solution.py:82
  226.6 5.3 %collective-permute-start.7 = (bf16[2,256,256]{1,2,0:T(8,128)(2,1)}, bf16[2,256,256]{1,2,0:T(8,128)(2,1)}, u32[]{:S(2)}, u32[]{:S(2)}) collective-permute-start(bf16[2,256,256]{1,2,0:T(8,128)(2,1)} %fusion.178), channel_id=1, source_target_pairs={{0,1},{1,2},{2,3},{3,4},{4,5},{5,6},{6,7},{8,9},{9,10},{10,11},{11... | collective-permute-start | bytes 786440 | tf_op jit(solution)/shard_map/ppermute | solution.py:23
  231.8 2.1 fusion.35
  238.6 2.1 fusion.36
  243.9 3.8 %multiply_reduce_fusion.1 = (f32[]{:T(128)}, f32[2,256,256]{1,2,0:T(8,128)}) fusion(f32[2,256,256]{1,2,0:T(8,128)} %get-tuple-element.6, f32[]{:T(128)} %sqrt.18, f32[2,256]{1,0:T(2,128)S(1)} %compare_convert_fusion, f32[2,256,256]{2,1,0:T(8,128)} %fusion.39, f32[2,256,256]{2,1,0:T(8,128)} %fusion.38, f32[2,256,256]{2,1,0:T(8,128)} %fusion.37, ...), kind=kOutput, calls=%fused_computation.77 | convolution fusion | flops 135659520 | bytes 4460552 | tf_op jit(solution)/shard_map/jab,jbc->jac/dot_general | solution.py:76
  247.7 20.0 %psum.70 = f32[]{:T(128)} all-reduce(f32[]{:T(128)} %get-tuple-element.17), channel_id=1, replica_groups=mesh['sec'=4,'blk'=8] {'blk'}, use_global_device_ids=true, to_apply=%region_15.0 | all-reduce | flops 1 | bytes 8 | tf_op jit(solution)/shard_map/psum | solution.py:80
  270.4 17.9 %psum.71 = f32[]{:T(128)} all-reduce(f32[]{:T(128)} %get-tuple-element.3), channel_id=1, replica_groups=mesh['sec'=4,'blk'=8] {'blk'}, use_global_device_ids=true, to_apply=%region_17.0 | all-reduce | flops 1 | bytes 8 | tf_op jit(solution)/shard_map/psum | solution.py:82
  291.8 23.5 %custom-call.9 = f32[2,128,128]{2,1,0:T(8,128)S(1)} custom-call(f32[2,128,128]{2,1,0:T(8,128)S(1)} %fusion.161), custom_call_target="Cholesky" | custom-call | tf_op jit(solution)/shard_map/vmap(jit(cholesky))/cholesky | solution.py:36
  315.5 19.7 %custom-call.10 = f32[2,1,128,128]{2,3,1,0:T(8,128)S(1)} custom-call(f32[2,1,128,128]{3,2,1,0:T(8,128)S(1)} %select_bitcast_fusion), custom_call_target="InvertDiagBlocksLowerTriangular" | custom-call | tf_op jit(solution)/shard_map/vmap()/triangular_solve | solution.py:39
  (71 shorter events, 50.6 us)
Async XLA Ops:
  0.6 288.4 %copy-start = (f32[1,2,256,128]{3,2,1,0:T(8,128)S(1)}, f32[1,2,256,128]{3,2,1,0:T(8,128)}, u32[]{:S(2)}) copy-start(f32[1,2,256,128]{3,2,1,0:T(8,128)} %param.11) | copy-start | bytes 786436
  0.6 37.6 %collective-permute-start = (bf16[1,6,2,256,256]{4,3,2,1,0:T(8,128)(2,1)}, bf16[1,6,2,256,256]{4,3,2,1,0:T(8,128)(2,1)S(1)}, u32[]{:S(2)}, u32[]{:S(2)}) collective-permute-start(bf16[1,6,2,256,256]{4,3,2,1,0:T(8,128)(2,1)} %param.6), channel_id=1, source_target_pairs={{24,0},{0,8},{8,16},{16,24},{25,1},{1,9},{9,17},{17,25},{26,2},{2,... | collective-permute-start | bytes 4718600 | tf_op jit(solution)/shard_map/ppermute | solution.py:12
  28.1 8.3 %collective-permute-start.2 = (bf16[2,256,256]{1,2,0:T(8,128)(2,1)S(1)}, bf16[2,256,256]{1,2,0:T(8,128)(2,1)S(1)}, u32[]{:S(2)}, u32[]{:S(2)}) collective-permute-start(bf16[2,256,256]{1,2,0:T(8,128)(2,1)S(1)} %fusion.106), channel_id=1, source_target_pairs={{1,0},{2,1},{3,2},{4,3},{5,4},{6,5},{7,6},{9,8},{10,9},{11,10},{12... | collective-permute-start | bytes 786440 | tf_op jit(solution)/shard_map/ppermute | solution.py:25
  29.4 8.8 %collective-permute-start.1 = (bf16[2,256,256]{1,2,0:T(8,128)(2,1)S(1)}, bf16[2,256,256]{1,2,0:T(8,128)(2,1)S(1)}, u32[]{:S(2)}, u32[]{:S(2)}) collective-permute-start(bf16[2,256,256]{1,2,0:T(8,128)(2,1)S(1)} %fusion.106), channel_id=1, source_target_pairs={{0,1},{1,2},{2,3},{3,4},{4,5},{5,6},{6,7},{8,9},{9,10},{10,11},{11... | collective-permute-start | bytes 786440 | tf_op jit(solution)/shard_map/ppermute | solution.py:23
  48.8 24.6 %copy-start.6 = (s32[1,2]{1,0:T(1,128)S(1)}, s32[1,2]{1,0:T(1,128)}, u32[]{:S(2)}) copy-start(s32[1,2]{1,0:T(1,128)} %param.10) | copy-start | bytes 28
  92.9 42.9 %copy-start.2 = (f32[2,256,256]{1,2,0:T(8,128)}, f32[2,256,256]{1,2,0:T(8,128)S(1)}, u32[]{:S(2)}) copy-start(f32[2,256,256]{1,2,0:T(8,128)S(1)} %get-tuple-element.10) | copy-start | bytes 1572868
  92.9 9.6 %collective-permute-start.4 = (bf16[2,256,256]{1,2,0:T(8,128)(2,1)}, bf16[2,256,256]{1,2,0:T(8,128)(2,1)S(1)}, u32[]{:S(2)}, u32[]{:S(2)}) collective-permute-start(bf16[2,256,256]{1,2,0:T(8,128)(2,1)} %get-tuple-element.9), channel_id=1, source_target_pairs={{1,0},{2,1},{3,2},{4,3},{5,4},{6,5},{7,6},{9,8},{10,9},{11,10},{12... | collective-permute-start | bytes 786440 | tf_op jit(solution)/shard_map/ppermute | solution.py:25
  94.3 11.6 %collective-permute-start.3 = (bf16[2,256,256]{1,2,0:T(8,128)(2,1)}, bf16[2,256,256]{1,2,0:T(8,128)(2,1)S(1)}, u32[]{:S(2)}, u32[]{:S(2)}) collective-permute-start(bf16[2,256,256]{1,2,0:T(8,128)(2,1)} %get-tuple-element.9), channel_id=1, source_target_pairs={{0,1},{1,2},{2,3},{3,4},{4,5},{5,6},{6,7},{8,9},{9,10},{10,11},{11... | collective-permute-start | bytes 786440 | tf_op jit(solution)/shard_map/ppermute | solution.py:23
  137.5 30.7 %copy-start.1 = (bf16[1,6,2,256,256]{4,3,2,1,0:T(8,128)(2,1)S(1)}, bf16[1,6,2,256,256]{4,3,2,1,0:T(8,128)(2,1)}, u32[]{:S(2)}) copy-start(bf16[1,6,2,256,256]{4,3,2,1,0:T(8,128)(2,1)} %param.7) | copy-start | bytes 4718596
  157.7 9.5 %collective-permute-start.6 = (bf16[2,256,256]{1,2,0:T(8,128)(2,1)}, bf16[2,256,256]{1,2,0:T(8,128)(2,1)}, u32[]{:S(2)}, u32[]{:S(2)}) collective-permute-start(bf16[2,256,256]{1,2,0:T(8,128)(2,1)} %fusion.179), channel_id=1, source_target_pairs={{1,0},{2,1},{3,2},{4,3},{5,4},{6,5},{7,6},{9,8},{10,9},{11,10},{12... | collective-permute-start | bytes 786440 | tf_op jit(solution)/shard_map/ppermute | solution.py:25
  159.6 10.6 %collective-permute-start.5 = (bf16[2,256,256]{1,2,0:T(8,128)(2,1)}, bf16[2,256,256]{1,2,0:T(8,128)(2,1)}, u32[]{:S(2)}, u32[]{:S(2)}) collective-permute-start(bf16[2,256,256]{1,2,0:T(8,128)(2,1)} %fusion.179), channel_id=1, source_target_pairs={{0,1},{1,2},{2,3},{3,4},{4,5},{5,6},{6,7},{8,9},{9,10},{10,11},{11... | collective-permute-start | bytes 786440 | tf_op jit(solution)/shard_map/ppermute | solution.py:23
  224.7 9.3 %collective-permute-start.8 = (bf16[2,256,256]{1,2,0:T(8,128)(2,1)}, bf16[2,256,256]{1,2,0:T(8,128)(2,1)}, u32[]{:S(2)}, u32[]{:S(2)}) collective-permute-start(bf16[2,256,256]{1,2,0:T(8,128)(2,1)} %fusion.178), channel_id=1, source_target_pairs={{1,0},{2,1},{3,2},{4,3},{5,4},{6,5},{7,6},{9,8},{10,9},{11,10},{12... | collective-permute-start | bytes 786440 | tf_op jit(solution)/shard_map/ppermute | solution.py:25
  226.6 10.4 %collective-permute-start.7 = (bf16[2,256,256]{1,2,0:T(8,128)(2,1)}, bf16[2,256,256]{1,2,0:T(8,128)(2,1)}, u32[]{:S(2)}, u32[]{:S(2)}) collective-permute-start(bf16[2,256,256]{1,2,0:T(8,128)(2,1)} %fusion.178), channel_id=1, source_target_pairs={{0,1},{1,2},{2,3},{3,4},{4,5},{5,6},{6,7},{8,9},{9,10},{10,11},{11... | collective-permute-start | bytes 786440 | tf_op jit(solution)/shard_map/ppermute | solution.py:23
  290.1 1.5 copy-start.3
  290.1 1.5 copy-start.5
  290.2 25.2 %copy-start.4 = (pred[128,128]{1,0:T(8,128)(4,1)S(1)}, pred[128,128]{1,0:T(8,128)(4,1)}, u32[]{:S(2)}) copy-start(pred[128,128]{1,0:T(8,128)(4,1)} %iota_compare_fusion.2) | copy-start | bytes 49156
where the time goes:
time: 340 us; the launch traced here: 339 us
  blocking collectives  175 us (51%)
  other arithmetic  59.7 us (18%)
  matrix products  58.2 us (17%)
  starting transfers between devices  26.5 us (8%)
  between operations  7.02 us (2%)
  local copies, waits for them, and re-layouts  6.37 us (2%)
  waiting for transfers between devices  5.83 us (2%)
    psum x4, blocking collectives, shards(): alpha = lax.psum(jnp.sum(vec * image), 'blk') / count  80.3 us
    psum x4, blocking collectives, shards(): resid_sq = lax.psum(jnp.sum(resid * resid), 'blk')  71.3 us
    dot_general x24, matrix products, shards(): jnp.einsum('jab,jbc->jac', left_terms[apply_k], mixed, preferred_element_...  53.7 us
    another operation x4, other arithmetic, project_block(): factor = jnp.linalg.cholesky(gram)  24.2 us
    psum x1, blocking collectives, shards(): start_sq = lax.psum(jnp.sum(vec * vec), 'blk')  23.3 us
    ppermute x4, starting transfers between devices, with_halo(): lax.ppermute(tail, axis, [(i, (i + 1) % count) for i in range(ends)])  20.9 us
    another operation x3, other arithmetic, project_block(): lax.linalg.triangular_solve(factor, inner, left_side=True, lower=True, tr...  20.4 us
    reduce_sum x4, other arithmetic, shards(): resid_sq = lax.psum(jnp.sum(resid * resid), 'blk')  7.46 us
  transfers between devices with their start and end apart: 9, of which 4 were waited for; matrix products, arithmetic and copies ran while one was open for 6% of the time, Pallas kernels for 0%

commit v1 on v0

v1 whole, which is shorter than its diff:
```python
import functools

import jax
import jax.numpy as jnp
from jax import lax
from jax.experimental import pallas as pl
from jax.experimental.pallas import tpu as pltpu
from jax.sharding import PartitionSpec as P

STEPS = 4
MESH = pl.DeviceIdType.MESH


def lanczos_kernel(
    n, nsec, count, dims_ref, left_ref, right_ref, psi_ref, vec_ref, coef_ref,
    left, own, low, high, prev, image, mask, mixed, row, rows, beta_ref,
    left_send, left_recv, halo_send, halo_recv, row_send, row_recv,
):
    blocks, side = psi_ref.shape[0], psi_ref.shape[1]
    terms = right_ref.shape[0]
    me = lax.axis_index("blk")
    sec = lax.axis_index("sec")
    after = lax.rem(sec + 1, nsec)
    before = lax.rem(sec + nsec - 1, nsec)

    barrier = pltpu.get_barrier_semaphore()

    def greet(o, carry):
        pl.semaphore_signal(barrier, inc=1, device_id={"blk": lax.rem(me + o, n)}, device_id_type=MESH)
        return carry

    lax.fori_loop(1, n, greet, 0)
    for other in (after, before):
        pl.semaphore_signal(barrier, inc=1, device_id={"sec": other}, device_id_type=MESH)
    pl.semaphore_wait(barrier, n + 1)

    left_copy = pltpu.make_async_remote_copy(
        src_ref=left_ref, dst_ref=left, send_sem=left_send, recv_sem=left_recv,
        device_id={"sec": after}, device_id_type=MESH,
    )
    left_copy.start()

    def row_copy(r, o, slot, target):
        return pltpu.make_async_remote_copy(
            src_ref=row.at[r], dst_ref=rows.at[r, slot],
            send_sem=row_send.at[r, o], recv_sem=row_recv.at[r, o],
            device_id={"blk": target}, device_id_type=MESH,
        )

    def exchange(r, sums):
        line = lax.broadcasted_iota(jnp.int32, (8, 128), 0)
        tile = jnp.zeros((8, 128), jnp.float32)
        for i, s in enumerate(sums):
            tile = jnp.where(line == i, s, tile)
        row[r] = tile
        rows[r, me] = tile

        def send(o, carry):
            row_copy(r, o, me, lax.rem(me + o, n)).start()
            return carry

        def take(o, carry):
            row_copy(r, o, lax.rem(me + n - o, n), lax.rem(me + o, n)).wait_recv()
            return carry

        lax.fori_loop(1, n, send, 0)
        lax.fori_loop(1, n, take, 0)
        return rows[r]

    def drain(r):
        def sent(o, carry):
            row_copy(r, o, me, lax.rem(me + o, n)).wait_send()
            return carry

        lax.fori_loop(1, n, sent, 0)

    def dot2(a, b):
        return jnp.sum(jnp.sum(a * b, axis=0), axis=(0, 1), keepdims=True)

    for q in range(blocks):
        d = dims_ref[q]
        inside = (lax.broadcasted_iota(jnp.int32, (side, side), 0) < d) & (
            lax.broadcasted_iota(jnp.int32, (side, side), 1) < d
        )
        mask[q] = inside.astype(jnp.float32)

    vec_ref[...] = psi_ref[...] * mask[...]
    prev[...] = jnp.zeros_like(prev)
    beta_ref[...] = jnp.zeros_like(beta_ref)

    @pl.when(me == 0)
    def _():
        low[...] = jnp.zeros_like(low)

    @pl.when(me == n - 1)
    def _():
        high[...] = jnp.zeros_like(high)

    got = exchange(0, [dot2(vec_ref[...], vec_ref[...])])
    start_sq = jnp.sum(got[:, 0:1, :], axis=0)[:, :1]
    vec_ref[...] = vec_ref[...] * jnp.sqrt(count / start_sq)
    drain(0)

    def step_body(step, carry):
        own[step] = vec_ref[...].astype(jnp.bfloat16)
        up = pltpu.make_async_remote_copy(
            src_ref=own.at[step], dst_ref=low.at[step],
            send_sem=halo_send.at[step, 0], recv_sem=halo_recv.at[step, 0],
            device_id={"blk": lax.rem(me + 1, n)}, device_id_type=MESH,
        )
        down = pltpu.make_async_remote_copy(
            src_ref=own.at[step], dst_ref=high.at[step],
            send_sem=halo_send.at[step, 1], recv_sem=halo_recv.at[step, 1],
            device_id={"blk": lax.rem(me + n - 1, n)}, device_id_type=MESH,
        )

        @pl.when(me < n - 1)
        def _():
            up.start()

        @pl.when(me > 0)
        def _():
            down.start()

        def mix(k, q, source):
            mixed[k, q] = lax.dot_general(
                source, right_ref[k, q], (((1,), (1,)), ((), ())), preferred_element_type=jnp.float32
            ).astype(jnp.bfloat16)

        def apply(ks, q):
            total = None
            for k in ks:
                part = jnp.dot(left[k, q], mixed[k, q], preferred_element_type=jnp.float32)
                total = part if total is None else total + part
            return total

        for q in range(blocks):
            mix(0, q, own[step, q])
            mix(1, q, own[step, q])

        @pl.when(me > 0)
        def _():
            up.wait_recv()

        @pl.when(me < n - 1)
        def _():
            down.wait_recv()

        for q in range(blocks):
            mix(2, q, low[step, q])
            mix(3, q, high[step, q])
            if q > 0:
                mix(4, q, low[step, q - 1])
            if q < blocks - 1:
                mix(5, q, high[step, q + 1])

        @pl.when(step == 0)
        def _():
            left_copy.wait()

        for q in range(blocks):
            ks = [0, 1, 2, 3] + ([4] if q > 0 else []) + ([5] if q < blocks - 1 else [])
            image[q] = apply(ks, q) * mask[q]

        beta = beta_ref[0:1, 0:1]
        vec = vec_ref[...]
        vw = dot2(vec, image[...])
        vv = dot2(vec, vec)
        image[...] = image[...] - beta * prev[...]
        vt = dot2(vec, image[...])
        mine = vt / jnp.where(vv > 0.0, vv, 1.0)
        rest = image[...] - mine * vec
        got = exchange(step + 1, [vw, mine, vv, dot2(rest, rest), dot2(rest, vec)])
        alpha = jnp.sum(got[:, 0:1, :], axis=0) / count
        gap = got[:, 1:2, :] - alpha[None]
        resid = jnp.sum(got[:, 3:4, :] + 2.0 * gap * got[:, 4:5, :] + gap * gap * got[:, 2:3, :], axis=0)
        next_beta = jnp.sqrt(jnp.maximum(resid, 0.0) / count + 1e-06)
        coef_ref[pl.ds(step, 1)] = alpha
        coef_ref[pl.ds(STEPS + step, 1)] = next_beta
        beta_ref[0:1] = next_beta
        vec = vec_ref[...]
        fresh = (image[...] - alpha[:, :1] * vec) * (1.0 / next_beta[:, :1])
        prev[...] = vec
        vec_ref[...] = fresh
        drain(step + 1)

        @pl.when(me < n - 1)
        def _():
            up.wait_send()

        @pl.when(me > 0)
        def _():
            down.wait_send()

        return carry

    lax.fori_loop(0, STEPS, step_body, 0)


def lanczos(left_built, right, psi, dims, n, nsec):
    blocks, side = psi.shape[0], psi.shape[1]
    terms = right.shape[0]
    count = float(n * blocks * side * side)
    vmem = pl.BlockSpec(memory_space=pltpu.VMEM)
    half = jnp.bfloat16
    return pl.pallas_call(
        functools.partial(lanczos_kernel, n, nsec, count),
        out_shape=(
            jax.ShapeDtypeStruct((blocks, side, side), jnp.float32),
            jax.ShapeDtypeStruct((2 * STEPS, 128), jnp.float32),
        ),
        in_specs=[pl.BlockSpec(memory_space=pltpu.SMEM), pl.BlockSpec(memory_space=pl.ANY), vmem, vmem],
        out_specs=(vmem, vmem),
        scratch_shapes=[
            pltpu.VMEM((terms, blocks, side, side), half),
            pltpu.VMEM((STEPS, blocks, side, side), half),
            pltpu.VMEM((STEPS, blocks, side, side), half),
            pltpu.VMEM((STEPS, blocks, side, side), half),
            pltpu.VMEM((blocks, side, side), jnp.float32),
            pltpu.VMEM((blocks, side, side), jnp.float32),
            pltpu.VMEM((blocks, side, side), jnp.float32),
            pltpu.VMEM((terms, blocks, side, side), half),
            pltpu.VMEM((STEPS + 1, 8, 128), jnp.float32),
            pltpu.VMEM((STEPS + 1, n, 8, 128), jnp.float32),
            pltpu.VMEM((8, 128), jnp.float32),
            pltpu.SemaphoreType.DMA,
            pltpu.SemaphoreType.DMA,
            pltpu.SemaphoreType.DMA((STEPS, 2)),
            pltpu.SemaphoreType.DMA((STEPS, 2)),
            pltpu.SemaphoreType.DMA((STEPS + 1, n)),
            pltpu.SemaphoreType.DMA((STEPS + 1, n)),
        ],
        compiler_params=pltpu.CompilerParams(
            collective_id=0, has_side_effects=True, vmem_limit_bytes=40 * 1024 * 1024
        ),
        name="lanczos",
    )(dims, left_built, right, psi)


def project_block(blockv, sketchb, cmask):
    hp = lax.Precision.HIGHEST
    ymat = jnp.dot(blockv, sketchb, precision=hp) * cmask[None, :]
    gram = jnp.dot(ymat.T, ymat, precision=hp) + jnp.diag(1.0 - cmask)
    factor = jnp.linalg.cholesky(gram)
    rhs = jnp.dot(ymat.T, blockv, precision=hp)
    inner = lax.linalg.triangular_solve(factor, rhs, left_side=True, lower=True)
    coef = lax.linalg.triangular_solve(factor, inner, left_side=True, lower=True, transpose_a=True)
    return jnp.dot(ymat, coef, precision=hp)


def shards(left_built, right_env, psi_init, block_dims, ranks, sketch):
    n = lax.axis_size("blk")
    nsec = lax.axis_size("sec")
    vec, coefs = lanczos(left_built[0], right_env[0], psi_init[0], block_dims[0], n, nsec)
    rmax = sketch.shape[3]
    cmask = (jnp.arange(rmax)[None, :] < ranks[0][:, None]).astype(jnp.float32)
    truncated = jax.vmap(project_block)(vec, sketch[0], cmask)
    return (truncated[None], coefs[:STEPS, 0][None], coefs[STEPS:, 0][None])


def solution(mesh):
    placed = (
        P("sec", None, "blk", None, None),
        P("sec", None, "blk", None, None),
        P("sec", "blk", None, None),
        P("sec", "blk"),
        P("sec", "blk"),
        P("sec", "blk", None, None),
    )
    return jax.shard_map(
        shards,
        mesh=mesh,
        in_specs=placed,
        out_specs=(P("sec", "blk", None, None), P("sec", None), P("sec", None)),
        check_vma=False,
    )
```

time: 340 us -> 136 us (0.40)
  blocking collectives: 175 us -> 0 us
  Pallas kernels: 0 us -> 82.1 us
  matrix products: 58.2 us -> 4.06 us
  starting transfers between devices: 26.5 us -> 0 us
  other arithmetic: 59.7 us -> 43.7 us
  between operations: 7.02 us -> 0.75 us
  waiting for transfers between devices: 5.83 us -> 0 us
    psum x9 -> x0, blocking collectives: 175 us -> none  [the longest x4 80.3 us: shards(): alpha = lax.psum(jnp.sum(vec * image), 'blk') / count]
    pallas_call x0 -> x1, Pallas kernels: none -> 82.1 us  [lanczos(): pl.pallas_call(functools.partial(lanczos_kernel, n, nsec, count), out_sha...]
    dot_general x24 -> x0, matrix products: 53.7 us -> none  [shards(): jnp.einsum('jab,jbc->jac', left_terms[apply_k], mixed, preferred_element_...]
    ppermute x9 -> x0, starting transfers between devices: 26.5 us -> none  [the longest x4 20.9 us: with_halo(): lax.ppermute(tail, axis, [(i, (i + 1) % count) for i in range(ends)])]
    reduce_sum x5 -> x0, other arithmetic: 8.27 us -> none  [the longest x4 7.46 us: shards(): resid_sq = lax.psum(jnp.sum(resid * resid), 'blk')]
    ppermute x9 -> x0, waiting for transfers between devices: 5.83 us -> none  [the longest x4 3.07 us: with_halo(): lax.ppermute(tail, axis, [(i, (i + 1) % count) for i in range(ends)])]
    convert_element_type x5 -> x0, other arithmetic: 5.36 us -> none  [the longest x4 4.63 us: shards(): ext = with_halo(vec.astype(jnp.bfloat16), (('blk', 0),), blocks)]
    slice x8 -> x1, local copies, waits for them, and re-layouts: 5 us -> 0.66 us  [shards(): return (truncated[None], coefs[:STEPS, 0][None], coefs[STEPS:, 0][None])]
  transfers between devices with their start and end apart: 9 -> 0, of which waited for: 4 -> 0; matrix products, arithmetic and copies ran while one was open for 6% -> 0% of each run, Pallas kernels for 0% -> 0%
where the time goes in v1:
time: 136 us
  Pallas kernels  82.1 us (60%)
  other arithmetic  43.7 us (32%)
  local copies, waits for them, and re-layouts  5.31 us (4%)
  matrix products  4.06 us (3%)
    pallas_call x1, Pallas kernels, lanczos(): pl.pallas_call(functools.partial(lanczos_kernel, n, nsec, count), out_sha...  82.1 us
    another operation x4, other arithmetic, project_block(): factor = jnp.linalg.cholesky(gram)  23.6 us
    another operation x3, other arithmetic, project_block(): lax.linalg.triangular_solve(factor, inner, left_side=True, lower=True, tr...  19.8 us
    unnamed x12, local copies, waits for them, and re-layouts  4.56 us

profile of v1, /device:TPU:0, one launch (start us, length us, event | category | flops | bytes accessed | tf_op | source)
XLA Modules:
  0.0 135.9 jit_solution(15765324784153061881)
XLA Ops:
  0.6 0.0 copy-start
  0.6 0.0 copy-start.1
  0.7 1.4 %copy-done.1 = bf16[1,6,2,256,256]{4,3,2,1,0:T(8,128)(2,1)S(1)} copy-done((bf16[1,6,2,256,256]{4,3,2,1,0:T(8,128)(2,1)S(1)}, bf16[1,6,2,256,256]{4,3,2,1,0:T(8,128)(2,1)}, u32[]{:S(2)}) %copy-start.1) | copy-done | bytes 1572888
  2.1 0.0 copy-start.2
  2.1 1.4 %copy-done.2 = bf16[1,6,2,256,256]{4,3,2,1,0:T(8,128)(2,1)S(1)} copy-done((bf16[1,6,2,256,256]{4,3,2,1,0:T(8,128)(2,1)S(1)}, bf16[1,6,2,256,256]{4,3,2,1,0:T(8,128)(2,1)}, u32[]{:S(2)}) %copy-start.2) | copy-done | bytes 1572888
  3.5 0.0 copy-start.3
  3.5 1.0 copy-done.3
  4.5 0.0 copy-start.4
  4.6 0.7 copy-done.4
  5.2 0.0 copy-start.5
  5.2 82.1 %lanczos.1 = (f32[2,256,256]{2,1,0:T(8,128)S(1)}, f32[8,128]{1,0:T(8,128)S(1)}) custom-call(s32[2]{0:T(128)S(1)} %bitcast.37, bf16[6,2,256,256]{3,2,1,0:T(8,128)(2,1)S(1)} %bitcast.34, bf16[6,2,256,256]{3,2,1,0:T(8,128)(2,1)S(1)} %bitcast.35, f32[2,256,256]{2,1,0:T(8,128)S(1)} %bitcast.36), custom_call_target="tpu_custom_call" | custom-call | tf_op jit(solution)/shard_map/lanczos/pallas_call | solution.py:206
  87.3 0.0 copy-done.5
  87.3 0.1 compare_convert_fusion
  87.4 0.0 copy-done
  87.4 0.6 convolution_multiply_fusion
  88.0 0.7 fusion.8
  88.7 0.6 fusion.7
  89.3 0.1 copy.14
  89.5 0.1 broadcast_subtract_fusion
  89.6 0.1 fusion.6
  89.7 23.5 %custom-call.9 = f32[2,128,128]{2,1,0:T(8,128)S(1)} custom-call(f32[2,128,128]{2,1,0:T(8,128)S(1)} %fusion.6), custom_call_target="Cholesky" | custom-call | tf_op jit(solution)/shard_map/vmap(jit(cholesky))/cholesky | solution.py:244
  113.2 0.1 compare_reduce_fusion
  113.3 0.1 select_bitcast_fusion
  113.4 19.7 %custom-call.10 = f32[2,1,128,128]{2,3,1,0:T(8,128)S(1)} custom-call(f32[2,1,128,128]{3,2,1,0:T(8,128)S(1)} %select_bitcast_fusion), custom_call_target="InvertDiagBlocksLowerTriangular" | custom-call | tf_op jit(solution)/shard_map/vmap()/triangular_solve | solution.py:247
  133.1 0.4 fusion.3
  133.5 0.4 fusion.1
  133.9 1.4 %convolution_bitcast_fusion = f32[1,2,256,256]{3,2,1,0:T(8,128)} fusion(f32[2,256,128]{2,1,0:T(8,128)S(1)} %convolution_multiply_fusion, f32[2,128,256]{2,1,0:T(8,128)S(1)} %fusion.1), kind=kOutput, calls=%fused_computation | convolution fusion | flops 201326592 | bytes 1048576 | tf_op jit(solution)/shard_map/vmap()/dot_general | solution.py:248
  135.2 0.7 slice_reduce_fusion
  (3 shorter events, 0.1 us)
Async XLA Ops:
  0.6 86.8 %copy-start = (f32[1,2,256,128]{3,2,1,0:T(8,128)S(1)}, f32[1,2,256,128]{3,2,1,0:T(8,128)}, u32[]{:S(2)}) copy-start(f32[1,2,256,128]{3,2,1,0:T(8,128)} %param.11) | copy-start | bytes 786436
  0.6 1.5 %copy-start.1 = (bf16[1,6,2,256,256]{4,3,2,1,0:T(8,128)(2,1)S(1)}, bf16[1,6,2,256,256]{4,3,2,1,0:T(8,128)(2,1)}, u32[]{:S(2)}) copy-start(bf16[1,6,2,256,256]{4,3,2,1,0:T(8,128)(2,1)} %param.6) | copy-start | bytes 4718596
  2.1 1.4 %copy-start.2 = (bf16[1,6,2,256,256]{4,3,2,1,0:T(8,128)(2,1)S(1)}, bf16[1,6,2,256,256]{4,3,2,1,0:T(8,128)(2,1)}, u32[]{:S(2)}) copy-start(bf16[1,6,2,256,256]{4,3,2,1,0:T(8,128)(2,1)} %param.7) | copy-start | bytes 4718596
  3.5 1.0 copy-start.3
  4.5 0.7 copy-start.4
  5.2 82.1 %copy-start.5 = (s32[1,2]{1,0:T(1,128)S(1)}, s32[1,2]{1,0:T(1,128)}, u32[]{:S(2)}) copy-start(s32[1,2]{1,0:T(1,128)} %param.10) | copy-start | bytes 28

commit v2 on v1

--- a/solution.py
+++ b/solution.py
@@ -237,24 +237,80 @@
     )(dims, left_built, right, psi)
 
 
-def project_block(blockv, sketchb, cmask):
+def project_kernel(ranks_ref, vec_ref, sketch_ref, out_ref, gram, side_rows):
+    blocks, side, rmax = sketch_ref.shape
     hp = lax.Precision.HIGHEST
-    ymat = jnp.dot(blockv, sketchb, precision=hp) * cmask[None, :]
-    gram = jnp.dot(ymat.T, ymat, precision=hp) + jnp.diag(1.0 - cmask)
-    factor = jnp.linalg.cholesky(gram)
-    rhs = jnp.dot(ymat.T, blockv, precision=hp)
-    inner = lax.linalg.triangular_solve(factor, rhs, left_side=True, lower=True)
-    coef = lax.linalg.triangular_solve(factor, inner, left_side=True, lower=True, transpose_a=True)
-    return jnp.dot(ymat, coef, precision=hp)
+
+    def mul(x, y, dims):
+        return lax.dot_general(x, y, (dims, ((), ())), precision=hp, preferred_element_type=jnp.float32)
+
+    line = lax.broadcasted_iota(jnp.int32, (rmax, rmax), 0)
+    lane = lax.broadcasted_iota(jnp.int32, (rmax, rmax), 1)
+    wide = lax.broadcasted_iota(jnp.int32, (rmax, side), 0)
+    for q in range(blocks):
+        rank = ranks_ref[q]
+        yt = mul(sketch_ref[q], vec_ref[q], ((0,), (1,)))
+        yt = jnp.where(wide < rank, yt, 0.0)
+        side_rows[q] = yt
+        extra = jnp.where((line == lane) & (line >= rank), 1.0, 0.0)
+        gram[q] = mul(yt, yt, ((1,), (1,))) + extra
+    sub = lax.broadcasted_iota(jnp.int32, (8, 1), 0)
+    for p in range(0, rmax, 8):
+        g = [gram[q, p : p + 8, :] for q in range(blocks)]
+        y = [side_rows[q, p : p + 8, :] for q in range(blocks)]
+        scale = [jnp.ones((8, 1), jnp.float32) for q in range(blocks)]
+        for j in range(8):
+            for q in range(blocks):
+                pivot = g[q][j : j + 1, p + j : p + j + 1]
+                factor = jnp.where(sub > j, g[q][:, p + j : p + j + 1], 0.0) / pivot
+                scale[q] = jnp.where(sub == j, pivot, scale[q])
+                y[q] = y[q] - factor * y[q][j : j + 1, :]
+                g[q] = g[q] - factor * g[q][j : j + 1, :]
+        for q in range(blocks):
+            norm = 1.0 / jnp.sqrt(scale[q])
+            g[q] = g[q] * norm
+            y[q] = y[q] * norm
+            side_rows[q, p : p + 8, :] = y[q]
+        if p + 8 < rmax:
+            flip = [g[q].T for q in range(blocks)]
+            for i in range(p + 8, rmax, 8):
+                for q in range(blocks):
+                    gi = gram[q, i : i + 8, :]
+                    yi = side_rows[q, i : i + 8, :]
+                    for j in range(8):
+                        f = flip[q][i : i + 8, j : j + 1]
+                        gi = gi - f * g[q][j : j + 1, :]
+                        yi = yi - f * y[q][j : j + 1, :]
+                    gram[q, i : i + 8, :] = gi
+                    side_rows[q, i : i + 8, :] = yi
+    for q in range(blocks):
+        z = side_rows[q]
+        out_ref[q] = mul(z, mul(z, vec_ref[q], ((1,), (0,))), ((0,), (0,)))
+
+
+def project(vec, sketch, ranks, **kw):
+    blocks, side, rmax = sketch.shape
+    vmem = pl.BlockSpec(memory_space=pltpu.VMEM)
+    return pl.pallas_call(
+        project_kernel,
+        out_shape=jax.ShapeDtypeStruct((blocks, side, side), jnp.float32),
+        in_specs=[pl.BlockSpec(memory_space=pltpu.SMEM), vmem, vmem],
+        out_specs=vmem,
+        scratch_shapes=[
+            pltpu.VMEM((blocks, rmax, rmax), jnp.float32),
+            pltpu.VMEM((blocks, rmax, side), jnp.float32),
+        ],
+        compiler_params=pltpu.CompilerParams(vmem_limit_bytes=32 * 1024 * 1024),
+        name="project",
+        **kw,
+    )(ranks, vec, sketch)
 
 
 def shards(left_built, right_env, psi_init, block_dims, ranks, sketch):
     n = lax.axis_size("blk")
     nsec = lax.axis_size("sec")
     vec, coefs = lanczos(left_built[0], right_env[0], psi_init[0], block_dims[0], n, nsec)
-    rmax = sketch.shape[3]
-    cmask = (jnp.arange(rmax)[None, :] < ranks[0][:, None]).astype(jnp.float32)
-    truncated = jax.vmap(project_block)(vec, sketch[0], cmask)
+    truncated = project(vec, sketch[0], ranks[0])
     return (truncated[None], coefs[:STEPS, 0][None], coefs[STEPS:, 0][None])
 
 

time: 136 us -> 107 us (0.79)
  other arithmetic: 43.7 us -> 0 us
  Pallas kernels: 82.1 us -> 101 us
  matrix products: 4.06 us -> 0 us
    another operation x7 -> x0, other arithmetic: 43.4 us -> none  [the longest x4 23.6 us: project_block(): factor = jnp.linalg.cholesky(gram)]
    pallas_call x0 -> x1, Pallas kernels: none -> 19.2 us  [project(): pl.pallas_call(project_kernel, out_shape=jax.ShapeDtypeStruct((blocks, si...]
    dot_general x4 -> x0, matrix products: 3.28 us -> none  [the longest x1 1.37 us: project_block(): return jnp.dot(ymat, coef, precision=hp)]
where the time goes in v2:
time: 107 us
  Pallas kernels  101 us (94%)
  local copies, waits for them, and re-layouts  5.17 us (5%)
    pallas_call x1, Pallas kernels, lanczos(): pl.pallas_call(functools.partial(lanczos_kernel, n, nsec, count), out_sha...  82.1 us
    pallas_call x1, Pallas kernels, project(): pl.pallas_call(project_kernel, out_shape=jax.ShapeDtypeStruct((blocks, si...  19.2 us
    unnamed x12, local copies, waits for them, and re-layouts  4.51 us

profile of v2, /device:TPU:0, one launch (start us, length us, event | category | flops | bytes accessed | tf_op | source)
XLA Modules:
  0.0 107.2 jit_solution(13846202358008233351)
XLA Ops:
  0.6 0.0 copy-start
  0.6 1.4 %copy-done = bf16[1,6,2,256,256]{4,3,2,1,0:T(8,128)(2,1)S(1)} copy-done((bf16[1,6,2,256,256]{4,3,2,1,0:T(8,128)(2,1)S(1)}, bf16[1,6,2,256,256]{4,3,2,1,0:T(8,128)(2,1)}, u32[]{:S(2)}) %copy-start) | copy-done | bytes 1572888
  2.0 0.0 copy-start.1
  2.0 1.4 %copy-done.1 = bf16[1,6,2,256,256]{4,3,2,1,0:T(8,128)(2,1)S(1)} copy-done((bf16[1,6,2,256,256]{4,3,2,1,0:T(8,128)(2,1)S(1)}, bf16[1,6,2,256,256]{4,3,2,1,0:T(8,128)(2,1)}, u32[]{:S(2)}) %copy-start.1) | copy-done | bytes 1572888
  3.4 0.0 copy-start.2
  3.5 1.0 copy-done.2
  4.5 0.0 copy-start.5
  4.5 0.7 copy-done.5
  5.1 0.0 copy-start.3
  5.1 0.0 copy-start.4
  5.2 82.1 %lanczos.1 = (f32[2,256,256]{2,1,0:T(8,128)S(1)}, f32[8,128]{1,0:T(8,128)S(1)}) custom-call(s32[2]{0:T(128)S(1)} %bitcast.14, bf16[6,2,256,256]{3,2,1,0:T(8,128)(2,1)S(1)} %bitcast.9, bf16[6,2,256,256]{3,2,1,0:T(8,128)(2,1)S(1)} %bitcast.10, f32[2,256,256]{2,1,0:T(8,128)S(1)} %bitcast.11), custom_call_target="tpu_custom_call" | custom-call | tf_op jit(solution)/shard_map/lanczos/pallas_call | solution.py:206
  87.3 0.7 slice_reduce_fusion
  87.9 0.0 copy-done.3
  87.9 0.0 copy-done.4
  88.0 19.2 %project.1 = f32[2,256,256]{2,1,0:T(8,128)} custom-call(s32[2]{0:T(128)S(1)} %bitcast.13, f32[2,256,256]{2,1,0:T(8,128)S(1)} %get-tuple-element.5.vec_ref, f32[2,256,128]{2,1,0:T(8,128)S(1)} %bitcast.12), custom_call_target="tpu_custom_call" | custom-call | tf_op jit(solution)/shard_map/project/pallas_call | solution.py:294
Async XLA Ops:
  0.6 1.4 %copy-start = (bf16[1,6,2,256,256]{4,3,2,1,0:T(8,128)(2,1)S(1)}, bf16[1,6,2,256,256]{4,3,2,1,0:T(8,128)(2,1)}, u32[]{:S(2)}) copy-start(bf16[1,6,2,256,256]{4,3,2,1,0:T(8,128)(2,1)} %param.6) | copy-start | bytes 4718596
  2.0 1.4 %copy-start.1 = (bf16[1,6,2,256,256]{4,3,2,1,0:T(8,128)(2,1)S(1)}, bf16[1,6,2,256,256]{4,3,2,1,0:T(8,128)(2,1)}, u32[]{:S(2)}) copy-start(bf16[1,6,2,256,256]{4,3,2,1,0:T(8,128)(2,1)} %param.7) | copy-start | bytes 4718596
  3.4 1.0 copy-start.2
  4.5 0.7 copy-start.5
  5.1 82.8 %copy-start.3 = (f32[1,2,256,128]{3,2,1,0:T(8,128)S(1)}, f32[1,2,256,128]{3,2,1,0:T(8,128)}, u32[]{:S(2)}) copy-start(f32[1,2,256,128]{3,2,1,0:T(8,128)} %param.11) | copy-start | bytes 786436
  5.1 82.8 %copy-start.4 = (s32[1,2]{1,0:T(1,128)S(1)}, s32[1,2]{1,0:T(1,128)}, u32[]{:S(2)}) copy-start(s32[1,2]{1,0:T(1,128)} %param.10) | copy-start | bytes 28

commit v3 on v2

--- a/solution.py
+++ b/solution.py
@@ -12,9 +12,9 @@
 
 
 def lanczos_kernel(
-    n, nsec, count, dims_ref, left_ref, right_ref, psi_ref, vec_ref, coef_ref,
-    left, own, low, high, prev, image, mask, mixed, row, rows, beta_ref,
-    left_send, left_recv, halo_send, halo_recv, row_send, row_recv,
+    n, nsec, count, dims_ref, left_ref, right_hbm, psi_hbm, vec_ref, coef_ref,
+    left, right_ref, psi_ref, own, near, far, prev, image, mask, mixed, row, rows, beta_ref,
+    load, left_send, left_recv, near_send, near_recv, far_send, far_recv, row_send, row_recv,
 ):
     blocks, side = psi_ref.shape[0], psi_ref.shape[1]
     terms = right_ref.shape[0]
@@ -23,6 +23,20 @@
     after = lax.rem(sec + 1, nsec)
     before = lax.rem(sec + nsec - 1, nsec)
 
+    odd = lax.rem(me, 2)
+    partner = me + 1 - 2 * odd
+    target = me + 2 - 4 * odd
+    source = me - 2 + 4 * odd
+    has_target = (target >= 0) & (target < n)
+    has_source = (source >= 0) & (source < n)
+    half = side // 2
+    chunks = [(b, h * half) for b in range(blocks) for h in range(2)]
+
+    psi_load = pltpu.make_async_copy(psi_hbm, psi_ref, load.at[0])
+    right_load = pltpu.make_async_copy(right_hbm, right_ref, load.at[1])
+    psi_load.start()
+    right_load.start()
+
     barrier = pltpu.get_barrier_semaphore()
 
     def greet(o, carry):
@@ -84,83 +98,89 @@
         )
         mask[q] = inside.astype(jnp.float32)
 
+    psi_load.wait()
     vec_ref[...] = psi_ref[...] * mask[...]
     prev[...] = jnp.zeros_like(prev)
     beta_ref[...] = jnp.zeros_like(beta_ref)
 
-    @pl.when(me == 0)
+    @pl.when(jnp.logical_not(has_source))
     def _():
-        low[...] = jnp.zeros_like(low)
-
-    @pl.when(me == n - 1)
-    def _():
-        high[...] = jnp.zeros_like(high)
+        far[...] = jnp.zeros_like(far)
 
     got = exchange(0, [dot2(vec_ref[...], vec_ref[...])])
     start_sq = jnp.sum(got[:, 0:1, :], axis=0)[:, :1]
     vec_ref[...] = vec_ref[...] * jnp.sqrt(count / start_sq)
     drain(0)
+    right_load.wait()
 
     def step_body(step, carry):
         own[step] = vec_ref[...].astype(jnp.bfloat16)
-        up = pltpu.make_async_remote_copy(
-            src_ref=own.at[step], dst_ref=low.at[step],
-            send_sem=halo_send.at[step, 0], recv_sem=halo_recv.at[step, 0],
-            device_id={"blk": lax.rem(me + 1, n)}, device_id_type=MESH,
-        )
-        down = pltpu.make_async_remote_copy(
-            src_ref=own.at[step], dst_ref=high.at[step],
-            send_sem=halo_send.at[step, 1], recv_sem=halo_recv.at[step, 1],
-            device_id={"blk": lax.rem(me + n - 1, n)}, device_id_type=MESH,
-        )
-
-        @pl.when(me < n - 1)
-        def _():
-            up.start()
-
-        @pl.when(me > 0)
-        def _():
-            down.start()
-
-        def mix(k, q, source):
+
+        def near_copy(c):
+            b, r = chunks[c]
+            return pltpu.make_async_remote_copy(
+                src_ref=own.at[step, b, pl.ds(r, half)], dst_ref=near.at[step, b, pl.ds(r, half)],
+                send_sem=near_send.at[step, c], recv_sem=near_recv.at[step, c],
+                device_id={"blk": partner}, device_id_type=MESH,
+            )
+
+        def far_copy(c):
+            b, r = chunks[c]
+            return pltpu.make_async_remote_copy(
+                src_ref=near.at[step, b, pl.ds(r, half)], dst_ref=far.at[step, b, pl.ds(r, half)],
+                send_sem=far_send.at[step, c], recv_sem=far_recv.at[step, c],
+                device_id={"blk": target}, device_id_type=MESH,
+            )
+
+        for c in range(len(chunks)):
+            near_copy(c).start()
+
+        def mix(k, q, block):
             mixed[k, q] = lax.dot_general(
-                source, right_ref[k, q], (((1,), (1,)), ((), ())), preferred_element_type=jnp.float32
+                block, right_ref[k, q], (((1,), (1,)), ((), ())), preferred_element_type=jnp.float32
             ).astype(jnp.bfloat16)
 
-        def apply(ks, q):
-            total = None
-            for k in ks:
-                part = jnp.dot(left[k, q], mixed[k, q], preferred_element_type=jnp.float32)
-                total = part if total is None else total + part
-            return total
+        def term(k, q):
+            return jnp.dot(left[k, q], mixed[k, q], preferred_element_type=jnp.float32)
 
         for q in range(blocks):
             mix(0, q, own[step, q])
             mix(1, q, own[step, q])
 
-        @pl.when(me > 0)
-        def _():
-            up.wait_recv()
-
-        @pl.when(me < n - 1)
-        def _():
-            down.wait_recv()
-
-        for q in range(blocks):
-            mix(2, q, low[step, q])
-            mix(3, q, high[step, q])
-            if q > 0:
-                mix(4, q, low[step, q - 1])
-            if q < blocks - 1:
-                mix(5, q, high[step, q + 1])
+        for c in range(len(chunks)):
+            near_copy(c).wait_recv()
+
+            @pl.when(has_target)
+            def _():
+                far_copy(c).start()
+
+        for q in range(blocks):
+            mix(3 - odd, q, near[step, q])
+        for i in range(blocks - 1):
+            mix(5 - odd, i + odd, near[step, i + 1 - odd])
 
         @pl.when(step == 0)
         def _():
             left_copy.wait()
 
         for q in range(blocks):
-            ks = [0, 1, 2, 3] + ([4] if q > 0 else []) + ([5] if q < blocks - 1 else [])
-            image[q] = apply(ks, q) * mask[q]
+            image[q] = term(0, q) + term(1, q) + term(3 - odd, q)
+        for i in range(blocks - 1):
+            image[i + odd] += term(5 - odd, i + odd)
+
+        @pl.when(has_source)
+        def _():
+            for c in range(len(chunks)):
+                far_copy(c).wait_recv()
+
+        for q in range(blocks):
+            mix(2 + odd, q, far[step, q])
+        for i in range(blocks - 1):
+            mix(4 + odd, i + 1 - odd, far[step, i + odd])
+        for i in range(blocks - 1):
+            image[i + 1 - odd] += term(4 + odd, i + 1 - odd)
+        for q in range(blocks):
+            image[q] = (image[q] + term(2 + odd, q)) * mask[q]
 
         beta = beta_ref[0:1, 0:1]
         vec = vec_ref[...]
@@ -184,13 +204,13 @@
         vec_ref[...] = fresh
         drain(step + 1)
 
-        @pl.when(me < n - 1)
+        for c in range(len(chunks)):
+            near_copy(c).wait_send()
+
+        @pl.when(has_target)
         def _():
-            up.wait_send()
-
-        @pl.when(me > 0)
-        def _():
-            down.wait_send()
+            for c in range(len(chunks)):
+                far_copy(c).wait_send()
 
         return carry
 
@@ -202,6 +222,7 @@
     terms = right.shape[0]
     count = float(n * blocks * side * side)
     vmem = pl.BlockSpec(memory_space=pltpu.VMEM)
+    any_place = pl.BlockSpec(memory_space=pl.ANY)
     half = jnp.bfloat16
     return pl.pallas_call(
         functools.partial(lanczos_kernel, n, nsec, count),
@@ -209,10 +230,12 @@
             jax.ShapeDtypeStruct((blocks, side, side), jnp.float32),
             jax.ShapeDtypeStruct((2 * STEPS, 128), jnp.float32),
         ),
-        in_specs=[pl.BlockSpec(memory_space=pltpu.SMEM), pl.BlockSpec(memory_space=pl.ANY), vmem, vmem],
+        in_specs=[pl.BlockSpec(memory_space=pltpu.SMEM), any_place, any_place, any_place],
         out_specs=(vmem, vmem),
         scratch_shapes=[
             pltpu.VMEM((terms, blocks, side, side), half),
+            pltpu.VMEM((terms, blocks, side, side), half),
+            pltpu.VMEM((blocks, side, side), jnp.float32),
             pltpu.VMEM((STEPS, blocks, side, side), half),
             pltpu.VMEM((STEPS, blocks, side, side), half),
             pltpu.VMEM((STEPS, blocks, side, side), half),
@@ -223,15 +246,18 @@
             pltpu.VMEM((STEPS + 1, 8, 128), jnp.float32),
             pltpu.VMEM((STEPS + 1, n, 8, 128), jnp.float32),
             pltpu.VMEM((8, 128), jnp.float32),
+            pltpu.SemaphoreType.DMA((2,)),
             pltpu.SemaphoreType.DMA,
             pltpu.SemaphoreType.DMA,
-            pltpu.SemaphoreType.DMA((STEPS, 2)),
-            pltpu.SemaphoreType.DMA((STEPS, 2)),
+            pltpu.SemaphoreType.DMA((STEPS, 2 * blocks)),
+            pltpu.SemaphoreType.DMA((STEPS, 2 * blocks)),
+            pltpu.SemaphoreType.DMA((STEPS, 2 * blocks)),
+            pltpu.SemaphoreType.DMA((STEPS, 2 * blocks)),
             pltpu.SemaphoreType.DMA((STEPS + 1, n)),
             pltpu.SemaphoreType.DMA((STEPS + 1, n)),
         ],
         compiler_params=pltpu.CompilerParams(
-            collective_id=0, has_side_effects=True, vmem_limit_bytes=40 * 1024 * 1024
+            collective_id=0, has_side_effects=True, vmem_limit_bytes=60 * 1024 * 1024
         ),
         name="lanczos",
     )(dims, left_built, right, psi)

time: 107 us -> 98.3 us (0.919)
  Pallas kernels: 101 us -> 94.9 us
  local copies, waits for them, and re-layouts: 5.17 us -> 2.47 us
    pallas_call x1, Pallas kernels: 82.1 us -> 75.7 us  [lanczos(): pl.pallas_call(functools.partial(lanczos_kernel, n, nsec, count), out_sha...]
    unnamed x12 -> x6, local copies, waits for them, and re-layouts: 4.51 us -> 1.05 us
where the time goes in v3:
time: 98.3 us; the launch traced here: 98 us
  Pallas kernels  94.9 us (97%)
  local copies, waits for them, and re-layouts  2.47 us (3%)
    pallas_call x1, Pallas kernels, lanczos(): pl.pallas_call(functools.partial(lanczos_kernel, n, nsec, count), out_sha...  75.7 us
    pallas_call x1, Pallas kernels, project(): pl.pallas_call(project_kernel, out_shape=jax.ShapeDtypeStruct((blocks, si...  19.2 us

profile of v3, /device:TPU:0, one launch (start us, length us, event | category | flops | bytes accessed | tf_op | source)
XLA Modules:
  0.0 98.0 jit_solution(1961083653493618110)
XLA Ops:
  0.6 0.0 copy-start.1
  0.6 0.0 copy-start.2
  0.7 75.7 %lanczos.1 = (f32[2,256,256]{2,1,0:T(8,128)}, f32[8,128]{1,0:T(8,128)}) custom-call(s32[2]{0:T(128)} %bitcast.17, bf16[6,2,256,256]{3,2,1,0:T(8,128)(2,1)} %bitcast.11, bf16[6,2,256,256]{3,2,1,0:T(8,128)(2,1)} %bitcast.12, f32[2,256,256]{2,1,0:T(8,128)} %bitcast.14), custom_call_target="tpu_custom_call" | custom-call | tf_op jit(solution)/shard_map/lanczos/pallas_call | solution.py:227
  76.3 1.4 %slice_reduce_fusion = (f32[4]{0:T(128)}, f32[4]{0:T(128)}) fusion(f32[8,128]{1,0:T(8,128)} %get-tuple-element.6), kind=kLoop, calls=%fused_computation | loop fusion | bytes 64 | tf_op jit(solution)/shard_map/slice | solution.py:340
  77.7 0.0 copy-done.1
  77.8 0.0 copy-done.2
  77.8 0.0 copy-start
  77.8 1.0 %copy-done = f32[2,256,256]{2,1,0:T(8,128)S(1)} copy-done((f32[2,256,256]{2,1,0:T(8,128)S(1)}, f32[2,256,256]{2,1,0:T(8,128)}, u32[]{:S(2)}) %copy-start) | copy-done | bytes 524312
  78.8 19.2 %project.1 = f32[2,256,256]{2,1,0:T(8,128)} custom-call(s32[2]{0:T(128)S(1)} %bitcast.10, f32[2,256,256]{2,1,0:T(8,128)S(1)} %copy-done, f32[2,256,128]{2,1,0:T(8,128)S(1)} %bitcast.9), custom_call_target="tpu_custom_call" | custom-call | tf_op jit(solution)/shard_map/project/pallas_call | solution.py:320
Async XLA Ops:
  0.6 77.1 %copy-start.1 = (f32[1,2,256,128]{3,2,1,0:T(8,128)S(1)}, f32[1,2,256,128]{3,2,1,0:T(8,128)}, u32[]{:S(2)}) copy-start(f32[1,2,256,128]{3,2,1,0:T(8,128)} %param.11) | copy-start | bytes 786436
  0.6 77.1 %copy-start.2 = (s32[1,2]{1,0:T(1,128)S(1)}, s32[1,2]{1,0:T(1,128)}, u32[]{:S(2)}) copy-start(s32[1,2]{1,0:T(1,128)} %param.10) | copy-start | bytes 28
  77.8 1.0 %copy-start = (f32[2,256,256]{2,1,0:T(8,128)S(1)}, f32[2,256,256]{2,1,0:T(8,128)}, u32[]{:S(2)}) copy-start(f32[2,256,256]{2,1,0:T(8,128)} %get-tuple-element.5.vec_ref) | copy-start | bytes 1572868

commit v4 on v3

--- a/solution.py
+++ b/solution.py
@@ -48,11 +48,17 @@
         pl.semaphore_signal(barrier, inc=1, device_id={"sec": other}, device_id_type=MESH)
     pl.semaphore_wait(barrier, n + 1)
 
-    left_copy = pltpu.make_async_remote_copy(
-        src_ref=left_ref, dst_ref=left, send_sem=left_send, recv_sem=left_recv,
-        device_id={"sec": after}, device_id_type=MESH,
-    )
-    left_copy.start()
+    order = [0, 1, 3 - odd, 5 - odd, 2 + odd, 4 + odd]
+
+    def left_copy(i):
+        return pltpu.make_async_remote_copy(
+            src_ref=left_ref.at[order[i]], dst_ref=left.at[order[i]],
+            send_sem=left_send.at[i], recv_sem=left_recv.at[i],
+            device_id={"sec": after}, device_id_type=MESH,
+        )
+
+    for i in range(len(order)):
+        left_copy(i).start()
 
     def row_copy(r, o, slot, target):
         return pltpu.make_async_remote_copy(
@@ -147,6 +153,18 @@
             mix(0, q, own[step, q])
             mix(1, q, own[step, q])
 
+        def apply_own():
+            for q in range(blocks):
+                image[q] = term(0, q) + term(1, q)
+
+        def left_wait(terms_of):
+            @pl.when(step == 0)
+            def _():
+                for i in terms_of:
+                    left_copy(i).wait()
+
+        pl.when(step > 0)(apply_own)
+
         for c in range(len(chunks)):
             near_copy(c).wait_recv()
 
@@ -159,12 +177,11 @@
         for i in range(blocks - 1):
             mix(5 - odd, i + odd, near[step, i + 1 - odd])
 
-        @pl.when(step == 0)
-        def _():
-            left_copy.wait()
-
-        for q in range(blocks):
-            image[q] = term(0, q) + term(1, q) + term(3 - odd, q)
+        left_wait((0, 1))
+        pl.when(step == 0)(apply_own)
+        left_wait((2, 3))
+        for q in range(blocks):
+            image[q] += term(3 - odd, q)
         for i in range(blocks - 1):
             image[i + odd] += term(5 - odd, i + odd)
 
@@ -177,6 +194,7 @@
             mix(2 + odd, q, far[step, q])
         for i in range(blocks - 1):
             mix(4 + odd, i + 1 - odd, far[step, i + odd])
+        left_wait((4, 5))
         for i in range(blocks - 1):
             image[i + 1 - odd] += term(4 + odd, i + 1 - odd)
         for q in range(blocks):
@@ -247,8 +265,8 @@
             pltpu.VMEM((STEPS + 1, n, 8, 128), jnp.float32),
             pltpu.VMEM((8, 128), jnp.float32),
             pltpu.SemaphoreType.DMA((2,)),
-            pltpu.SemaphoreType.DMA,
-            pltpu.SemaphoreType.DMA,
+            pltpu.SemaphoreType.DMA((terms,)),
+            pltpu.SemaphoreType.DMA((terms,)),
             pltpu.SemaphoreType.DMA((STEPS, 2 * blocks)),
             pltpu.SemaphoreType.DMA((STEPS, 2 * blocks)),
             pltpu.SemaphoreType.DMA((STEPS, 2 * blocks)),
@@ -280,22 +298,24 @@
         side_rows[q] = yt
         extra = jnp.where((line == lane) & (line >= rank), 1.0, 0.0)
         gram[q] = mul(yt, yt, ((1,), (1,))) + extra
-    sub = lax.broadcasted_iota(jnp.int32, (8, 1), 0)
+    sub = lax.broadcasted_iota(jnp.int32, (8, rmax), 0)
     for p in range(0, rmax, 8):
         g = [gram[q, p : p + 8, :] for q in range(blocks)]
         y = [side_rows[q, p : p + 8, :] for q in range(blocks)]
-        scale = [jnp.ones((8, 1), jnp.float32) for q in range(blocks)]
+        scale = [jnp.ones((8, rmax), jnp.float32) for q in range(blocks)]
         for j in range(8):
             for q in range(blocks):
-                pivot = g[q][j : j + 1, p + j : p + j + 1]
-                factor = jnp.where(sub > j, g[q][:, p + j : p + j + 1], 0.0) / pivot
+                column = jnp.broadcast_to(g[q][:, p + j : p + j + 1], (8, rmax))
+                pivot = jnp.broadcast_to(column[j : j + 1, :], (8, rmax))
+                factor = jnp.where(sub > j, column, 0.0) * (1.0 / pivot)
                 scale[q] = jnp.where(sub == j, pivot, scale[q])
-                y[q] = y[q] - factor * y[q][j : j + 1, :]
+                wide_factor = jnp.concatenate([factor] * (side // rmax), axis=1)
+                y[q] = y[q] - wide_factor * y[q][j : j + 1, :]
                 g[q] = g[q] - factor * g[q][j : j + 1, :]
         for q in range(blocks):
             norm = 1.0 / jnp.sqrt(scale[q])
             g[q] = g[q] * norm
-            y[q] = y[q] * norm
+            y[q] = y[q] * jnp.concatenate([norm] * (side // rmax), axis=1)
             side_rows[q, p : p + 8, :] = y[q]
         if p + 8 < rmax:
             flip = [g[q].T for q in range(blocks)]

time: 98.3 us -> 101 us (1.027)
  Pallas kernels: 94.9 us -> 97.3 us
    pallas_call x1, Pallas kernels: 19.2 us -> 22.3 us  [project(): pl.pallas_call(project_kernel, out_shape=jax.ShapeDtypeStruct((blocks, si...]
where the time goes in v4:
time: 101 us; the launch traced here: 100 us
  Pallas kernels  97.3 us (96%)
  local copies, waits for them, and re-layouts  2.47 us (2%)
    pallas_call x1, Pallas kernels, lanczos(): pl.pallas_call(functools.partial(lanczos_kernel, n, nsec, count), out_sha...  75 us
    pallas_call x1, Pallas kernels, project(): pl.pallas_call(project_kernel, out_shape=jax.ShapeDtypeStruct((blocks, si...  22.3 us

profile of v4, /device:TPU:0, one launch (start us, length us, event | category | flops | bytes accessed | tf_op | source)
XLA Modules:
  0.0 100.5 jit_solution(7410255445798544161)
XLA Ops:
  0.6 0.0 copy-start.1
  0.6 0.0 copy-start.2
  0.7 75.0 %lanczos.1 = (f32[2,256,256]{2,1,0:T(8,128)}, f32[8,128]{1,0:T(8,128)}) custom-call(s32[2]{0:T(128)} %bitcast.17, bf16[6,2,256,256]{3,2,1,0:T(8,128)(2,1)} %bitcast.11, bf16[6,2,256,256]{3,2,1,0:T(8,128)(2,1)} %bitcast.12, f32[2,256,256]{2,1,0:T(8,128)} %bitcast.14), custom_call_target="tpu_custom_call" | custom-call | tf_op jit(solution)/shard_map/lanczos/pallas_call | solution.py:245
  75.7 1.4 %slice_reduce_fusion = (f32[4]{0:T(128)}, f32[4]{0:T(128)}) fusion(f32[8,128]{1,0:T(8,128)} %get-tuple-element.6), kind=kLoop, calls=%fused_computation | loop fusion | bytes 64 | tf_op jit(solution)/shard_map/slice | solution.py:360
  77.1 0.0 copy-done.1
  77.1 0.0 copy-done.2
  77.1 0.0 copy-start
  77.1 1.0 %copy-done = f32[2,256,256]{2,1,0:T(8,128)S(1)} copy-done((f32[2,256,256]{2,1,0:T(8,128)S(1)}, f32[2,256,256]{2,1,0:T(8,128)}, u32[]{:S(2)}) %copy-start) | copy-done | bytes 524312
  78.2 22.3 %project.1 = f32[2,256,256]{2,1,0:T(8,128)} custom-call(s32[2]{0:T(128)S(1)} %bitcast.10, f32[2,256,256]{2,1,0:T(8,128)S(1)} %copy-done, f32[2,256,128]{2,1,0:T(8,128)S(1)} %bitcast.9), custom_call_target="tpu_custom_call" | custom-call | tf_op jit(solution)/shard_map/project/pallas_call | solution.py:340
Async XLA Ops:
  0.6 76.5 %copy-start.1 = (f32[1,2,256,128]{3,2,1,0:T(8,128)S(1)}, f32[1,2,256,128]{3,2,1,0:T(8,128)}, u32[]{:S(2)}) copy-start(f32[1,2,256,128]{3,2,1,0:T(8,128)} %param.11) | copy-start | bytes 786436
  0.6 76.5 %copy-start.2 = (s32[1,2]{1,0:T(1,128)S(1)}, s32[1,2]{1,0:T(1,128)}, u32[]{:S(2)}) copy-start(s32[1,2]{1,0:T(1,128)} %param.10) | copy-start | bytes 28
  77.1 1.0 %copy-start = (f32[2,256,256]{2,1,0:T(8,128)S(1)}, f32[2,256,256]{2,1,0:T(8,128)}, u32[]{:S(2)}) copy-start(f32[2,256,256]{2,1,0:T(8,128)} %get-tuple-element.5.vec_ref) | copy-start | bytes 1572868

commit v5 on v4

--- a/solution.py
+++ b/solution.py
@@ -298,24 +298,22 @@
         side_rows[q] = yt
         extra = jnp.where((line == lane) & (line >= rank), 1.0, 0.0)
         gram[q] = mul(yt, yt, ((1,), (1,))) + extra
-    sub = lax.broadcasted_iota(jnp.int32, (8, rmax), 0)
+    sub = lax.broadcasted_iota(jnp.int32, (8, 1), 0)
     for p in range(0, rmax, 8):
         g = [gram[q, p : p + 8, :] for q in range(blocks)]
         y = [side_rows[q, p : p + 8, :] for q in range(blocks)]
-        scale = [jnp.ones((8, rmax), jnp.float32) for q in range(blocks)]
+        scale = [jnp.ones((8, 1), jnp.float32) for q in range(blocks)]
         for j in range(8):
             for q in range(blocks):
-                column = jnp.broadcast_to(g[q][:, p + j : p + j + 1], (8, rmax))
-                pivot = jnp.broadcast_to(column[j : j + 1, :], (8, rmax))
-                factor = jnp.where(sub > j, column, 0.0) * (1.0 / pivot)
+                pivot = g[q][j : j + 1, p + j : p + j + 1]
+                factor = jnp.where(sub > j, g[q][:, p + j : p + j + 1], 0.0) / pivot
                 scale[q] = jnp.where(sub == j, pivot, scale[q])
-                wide_factor = jnp.concatenate([factor] * (side // rmax), axis=1)
-                y[q] = y[q] - wide_factor * y[q][j : j + 1, :]
+                y[q] = y[q] - factor * y[q][j : j + 1, :]
                 g[q] = g[q] - factor * g[q][j : j + 1, :]
         for q in range(blocks):
             norm = 1.0 / jnp.sqrt(scale[q])
             g[q] = g[q] * norm
-            y[q] = y[q] * jnp.concatenate([norm] * (side // rmax), axis=1)
+            y[q] = y[q] * norm
             side_rows[q, p : p + 8, :] = y[q]
         if p + 8 < rmax:
             flip = [g[q].T for q in range(blocks)]

time: 101 us -> 97.6 us (0.966)
  Pallas kernels: 97.3 us -> 94.3 us
    pallas_call x1, Pallas kernels: 22.3 us -> 19.2 us  [project(): pl.pallas_call(project_kernel, out_shape=jax.ShapeDtypeStruct((blocks, si...]
where the time goes in v5:
time: 97.6 us; the launch traced here: 97.4 us
  Pallas kernels  94.3 us (97%)
  local copies, waits for them, and re-layouts  2.47 us (3%)
    pallas_call x1, Pallas kernels, lanczos(): pl.pallas_call(functools.partial(lanczos_kernel, n, nsec, count), out_sha...  75 us
    pallas_call x1, Pallas kernels, project(): pl.pallas_call(project_kernel, out_shape=jax.ShapeDtypeStruct((blocks, si...  19.2 us

profile of v5, /device:TPU:0, one launch (start us, length us, event | category | flops | bytes accessed | tf_op | source)
XLA Modules:
  0.0 97.4 jit_solution(5991088260003431403)
XLA Ops:
  0.6 0.0 copy-start.1
  0.6 0.0 copy-start.2
  0.7 75.0 %lanczos.1 = (f32[2,256,256]{2,1,0:T(8,128)}, f32[8,128]{1,0:T(8,128)}) custom-call(s32[2]{0:T(128)} %bitcast.17, bf16[6,2,256,256]{3,2,1,0:T(8,128)(2,1)} %bitcast.11, bf16[6,2,256,256]{3,2,1,0:T(8,128)(2,1)} %bitcast.12, f32[2,256,256]{2,1,0:T(8,128)} %bitcast.14), custom_call_target="tpu_custom_call" | custom-call | tf_op jit(solution)/shard_map/lanczos/pallas_call | solution.py:245
  75.7 1.4 %slice_reduce_fusion = (f32[4]{0:T(128)}, f32[4]{0:T(128)}) fusion(f32[8,128]{1,0:T(8,128)} %get-tuple-element.6), kind=kLoop, calls=%fused_computation | loop fusion | bytes 64 | tf_op jit(solution)/shard_map/slice | solution.py:358
  77.1 0.0 copy-done.1
  77.1 0.0 copy-done.2
  77.1 0.0 copy-start
  77.1 1.0 %copy-done = f32[2,256,256]{2,1,0:T(8,128)S(1)} copy-done((f32[2,256,256]{2,1,0:T(8,128)S(1)}, f32[2,256,256]{2,1,0:T(8,128)}, u32[]{:S(2)}) %copy-start) | copy-done | bytes 524312
  78.2 19.2 %project.1 = f32[2,256,256]{2,1,0:T(8,128)} custom-call(s32[2]{0:T(128)S(1)} %bitcast.10, f32[2,256,256]{2,1,0:T(8,128)S(1)} %copy-done, f32[2,256,128]{2,1,0:T(8,128)S(1)} %bitcast.9), custom_call_target="tpu_custom_call" | custom-call | tf_op jit(solution)/shard_map/project/pallas_call | solution.py:338
Async XLA Ops:
  0.6 76.5 %copy-start.1 = (f32[1,2,256,128]{3,2,1,0:T(8,128)S(1)}, f32[1,2,256,128]{3,2,1,0:T(8,128)}, u32[]{:S(2)}) copy-start(f32[1,2,256,128]{3,2,1,0:T(8,128)} %param.11) | copy-start | bytes 786436
  0.6 76.5 %copy-start.2 = (s32[1,2]{1,0:T(1,128)S(1)}, s32[1,2]{1,0:T(1,128)}, u32[]{:S(2)}) copy-start(s32[1,2]{1,0:T(1,128)} %param.10) | copy-start | bytes 28
  77.1 1.0 %copy-start = (f32[2,256,256]{2,1,0:T(8,128)S(1)}, f32[2,256,256]{2,1,0:T(8,128)}, u32[]{:S(2)}) copy-start(f32[2,256,256]{2,1,0:T(8,128)} %get-tuple-element.5.vec_ref) | copy-start | bytes 1572868
